TPU v7x, 32 devices: a whole 2x2x4 slice. The times are simulated.
32 devices in a mesh: section: 4 (over z), dp: 2 (over core), tensor: 4 (over y, x).
Axes of the slice: x: 2, y: 2, z: 4, core: 2. Of those that a mesh axis runs over, the one named last changes fastest.
Arguments:
- patches: bfloat16 [6144, 1280], P(('section', 'dp')), may hold values from -6 to 6
- window_ids: int32 [6144], P(('section', 'dp')), may hold values from 0 to 152, never falling along the last dimension, each value on 1 to 64 neighbouring positions
- norm_gain: float32 [1280], replicated, may hold values from 0.25 to 1.75
- w_qkv: bfloat16 [1280, 3, 1280], P(('section', 'dp'), None, 'tensor'), may hold values from -0.15625 to 0.15625
- qkv_bias: float32 [3, 1280], P(None, 'tensor'), may hold values from -10 to 10
- w_out: bfloat16 [1280, 1280], P(('section', 'dp'), 'tensor'), may hold values from -0.15625 to 0.15625
Outputs:
- mixed: bfloat16 [6144, 1280], P(('section', 'dp'))
Inputs may be any that keep to these rules, and one draw needn't show every extreme that they name: window_ids never fall along the packed order; each window holds 1 to 64 consecutive patches, and some window holds exactly 64.
All inputs are finite; a program needn't handle non-finite values.
Results may differ from a plain program's by a relative error of at most 0.012.
Values may be sent and summed in bfloat16 or wider, within the bound.
A program may use at most 64 MiB of HBM per device.

v0:
```python
import jax
import jax.numpy as jnp
from jax import lax
from jax.sharding import PartitionSpec as P

HEAD = 80
WIN = 64


def with_halo(cells, sides, width):
    for axis, dim in sides:
        count = lax.axis_size(axis)
        ends = count - 1
        head = lax.slice_in_dim(cells, 0, width, axis=dim)
        tail = lax.slice_in_dim(cells, cells.shape[dim] - width, cells.shape[dim], axis=dim)
        cells = jnp.concatenate(
            [
                lax.ppermute(tail, axis, [(i, (i + 1) % count) for i in range(ends)]),
                cells,
                lax.ppermute(head, axis, [((i + 1) % count, i) for i in range(ends)]),
            ],
            axis=dim,
        )
    return cells


def local(patches, window_ids, norm_gain, w_qkv, qkv_bias, w_out):
    rows = patches.shape[0]
    local_cols = w_qkv.shape[2]
    local_heads = local_cols // HEAD
    values_f = patches.astype(jnp.float32)
    scale_row = lax.rsqrt(jnp.mean(values_f * values_f, axis=-1, keepdims=True) + 1e-06)
    normed = (values_f * scale_row * norm_gain).astype(jnp.bfloat16)
    piece = lax.all_gather(w_qkv, ("section", "dp"), axis=0, tiled=True)
    count = piece.shape[0]
    proj = jnp.dot(normed, piece.reshape(count, 3 * local_cols), preferred_element_type=jnp.float32)
    proj = (proj + qkv_bias.reshape(3 * local_cols)).astype(jnp.bfloat16)
    keyvals = with_halo(proj[:, local_cols:], ((("section", "dp"), 0),), WIN)
    marks = with_halo(window_ids + 1, ((("section", "dp"), 0),), WIN)
    block_rows = 128
    blocks = rows // block_rows
    key_span = block_rows + 2 * WIN
    queries = proj[:, :local_cols].reshape(blocks, block_rows, local_heads, HEAD)
    kv_blocks = jnp.stack(
        [keyvals[i * block_rows : i * block_rows + key_span] for i in range(blocks)]
    )
    mark_blocks = jnp.stack(
        [marks[i * block_rows : i * block_rows + key_span] for i in range(blocks)]
    )
    keys = kv_blocks[:, :, :local_cols].reshape(blocks, key_span, local_heads, HEAD)
    vals = kv_blocks[:, :, local_cols:].reshape(blocks, key_span, local_heads, HEAD)
    mark_q = marks[WIN : WIN + rows].reshape(blocks, block_rows)
    allowed = mark_q[:, :, None] == mark_blocks[:, None, :]
    factor = 1.0 / HEAD**0.5
    scores = (
        jnp.einsum("bqhd,bkhd->bhqk", queries, keys, preferred_element_type=jnp.float32) * factor
    )
    scores = jnp.where(allowed[:, None], scores, jnp.float32(-1e30))
    top = jnp.max(scores, axis=-1, keepdims=True)
    expo = jnp.where(allowed[:, None], jnp.exp(scores - top), jnp.float32(0.0))
    probs = (expo / jnp.sum(expo, axis=-1, keepdims=True)).astype(jnp.bfloat16)
    attn = jnp.einsum("bhqk,bkhd->bqhd", probs, vals, preferred_element_type=jnp.float32)
    attn = attn.reshape(rows, local_cols).astype(jnp.bfloat16)
    partial_out = lax.dot_general(
        attn,
        lax.all_gather(w_out, ("section", "dp"), axis=0, tiled=True),
        (((1,), (1,)), ((), ())),
        preferred_element_type=jnp.float32,
    )
    summed = lax.psum(partial_out.astype(jnp.bfloat16), "tensor").astype(jnp.float32)
    return (values_f + summed).astype(jnp.bfloat16)


def solution(mesh):
    placed = (
        P(("section", "dp"), None),
        P(("section", "dp")),
        P(),
        P(("section", "dp"), None, "tensor"),
        P(None, "tensor"),
        P(("section", "dp"), "tensor"),
    )
    return jax.shard_map(
        local, mesh=mesh, in_specs=placed, out_specs=P(("section", "dp"), None), check_vma=False
    )
```

profile of v0, /device:TPU:0, one launch (start us, length us, event | category | flops | bytes accessed | tf_op | source)
XLA Modules:
  0.0 164.3 jit_solution(382785309299708029)
XLA Ops:
  6.5 0.0 copy-start.5
  6.5 0.0 all-gather.2.cloned.1.call-start
  6.5 0.7 all-gather.2.cloned.1.call-update
  7.3 0.0 all-reduce.2.cloned.1.call-start
  7.3 0.7 fusion.32
  8.0 0.1 fusion.35
  8.1 2.3 %collective-permute-start.2 = (s32[64]{0:T(128)S(1)}, s32[64]{0:T(128)S(1)}, u32[]{:S(2)}, u32[]{:S(2)}) collective-permute-start(s32[64]{0:T(128)S(1)} %get-tuple-element.14), channel_id=1, source_target_pairs={{0,4},{4,8},{8,12},{12,16},{16,20},{20,24},{24,28},{1,5},{5,9},{9,... | collective-permute-start | bytes 776 | tf_op jit(solution)/shard_map/ppermute | solution.py:18
  10.4 1.3 collective-permute-start.3
  11.7 0.1 fusion.36
  11.8 2.0 %fusion.1 = f32[768]{0:T(1024)S(1)} fusion(bf16[768,1280]{1,0:T(8,128)(2,1)} %param.6), kind=kLoop, calls=%fused_computation.4 | loop fusion | flops 2948352 | bytes 1969152 | tf_op jit(solution)/shard_map/reduce_sum | solution.py:32
  13.8 27.3 %all_gather.7 = bf16[1280,320]{1,0:T(8,128)(2,1)} all-gather(bf16[160,320]{1,0:T(8,128)(2,1)} %param.11), channel_id=1, replica_groups=mesh['section'=4,'dp'=2,'tensor'=4] {'section','dp'}, dimensions={0}, use_global_device_ids=true | all-gather | bytes 921600 | tf_op jit(solution)/shard_map/all_gather | solution.py:66
  41.1 0.0 copy-done.5
  41.1 0.1 add.34
  41.2 0.0 collective-permute-done.2
  41.2 0.0 collective-permute-done.3
  41.2 0.1 pad_add_fusion.1
  41.3 0.1 slice.87
  41.4 0.0 copy-start
  41.4 0.0 copy-start.6
  41.4 14.1 %all-gather.2.cloned.1.call-done = bf16[1280,3,320]{2,0,1:T(8,128)(2,1)} async-done(((bf16[160,3,320]{2,0,1:T(8,128)(2,1)}), bf16[1280,3,320]{2,0,1:T(8,128)(2,1)}) %all-gather.2.cloned.1.call-update) | async-done | bytes 2457616 | tf_op jit(solution)/shard_map/all_gather | solution.py:34
  55.5 5.3 %copy.11 = bf16[1280,3,320]{0,2,1:T(8,128)(2,1)} copy(bf16[1280,3,320]{2,0,1:T(8,128)(2,1)} %all-gather.2.cloned.1.call-done) | data formatting | bytes 4915200 | tf_op jit(solution)/shard_map/all_gather | solution.py:34
  60.8 0.0 copy-done
  60.8 0.0 copy-done.6
  60.8 3.9 %add_convert_fusion = bf16[768,960]{0,1:T(8,128)(2,1)S(1)} fusion(bf16[1280,960]{0,1:T(8,128)(2,1)} %bitcast.51, bf16[768,1280]{1,0:T(8,128)(2,1)S(1)} %copy-done, f32[1280]{0:T(1024)S(1)} %copy-done.6, f32[768]{0:T(1024)S(1)} %add_rsqrt_fusion, f32[960]{0:T(1024)S(1)} %add.34), kind=kOutput, calls=%fused_computation.12 | convolution fusion | flops 1892843520 | bytes 5910272 | tf_op jit(solution)/shard_map/dot_general | solution.py:36
  64.7 0.0 copy-start.1
  64.7 0.9 fusion.34
  65.6 2.8 %collective-permute-start = (bf16[64,640]{0,1:T(8,128)(2,1)}, bf16[64,640]{0,1:T(8,128)(2,1)}, u32[]{:S(2)}, u32[]{:S(2)}) collective-permute-start(bf16[64,640]{0,1:T(8,128)(2,1)} %get-tuple-element.8), channel_id=1, source_target_pairs={{0,4},{4,8},{8,12},{12,16},{16,20},{20,24},{24,28},{1,5},{5,9},{9,... | collective-permute-start | bytes 245768 | tf_op jit(solution)/shard_map/ppermute | solution.py:18
  68.4 0.9 broadcast_compare_fusion
  69.3 0.1 slice.91
  69.3 0.0 copy-done.1
  69.4 1.3 collective-permute-start.1
  70.7 1.4 reshape.31
  72.1 0.0 collective-permute-done
  72.1 1.1 fusion.29
  73.2 1.2 fusion.27
  74.4 1.2 fusion.26
  75.6 1.2 fusion.25
  76.8 1.2 fusion.24
  78.0 0.0 copy-start.2
  78.0 0.0 collective-permute-done.1
  78.0 1.2 fusion.23
  79.2 0.1 fusion.33
  79.3 0.0 copy-start.4
  79.3 0.0 copy-done.2
  79.3 0.6 fusion.20
  80.0 0.3 copy-done.4
  80.3 1.8 %fusion.37 = (f32[6,4,128]{2,1,0:T(4,128)S(1)}, f32[6,4,128,256]{3,2,1,0:T(8,128)S(1)}) fusion(f32[6,4,128,256]{3,2,1,0:T(8,128)S(1)} %fusion.20, pred[6,128,256]{2,1,0:T(8,128)(4,1)S(1)} %copy-done.4), kind=kOutput, calls=%fused_computation.53 | output fusion | flops 5505279 | bytes 6500352 | tf_op jit(solution)/shard_map/sub | solution.py:60
  82.0 0.0 copy-start.3
  82.0 0.8 fusion.17
  82.8 0.3 copy.13
  83.1 0.1 copy-done.3
  83.2 2.5 %convolution_convert_fusion = bf16[768,1280]{1,0:T(8,128)(2,1)} fusion(bf16[1280,320]{1,0:T(8,128)(2,1)S(1)} %copy-done.3, bf16[40,8,6,128]{3,2,1,0:T(8,128)(2,1)S(1)} %bitcast.53), kind=kOutput, calls=%fused_computation.8 | convolution fusion | flops 630128640 | bytes 3276800 | tf_op jit(solution)/shard_map/dot_general | solution.py:64
  85.7 0.0 all-reduce.2.cloned.1.call-update
  85.7 68.4 %all-reduce.2.cloned.1.call-done = bf16[768,1280]{1,0:T(8,128)(2,1)} async-done(((bf16[768,1280]{1,0:T(8,128)(2,1)}), bf16[768,1280]{1,0:T(8,128)(2,1)}) %all-reduce.2.cloned.1.call-update) | async-done | bytes 1966096 | tf_op jit(solution)/shard_map/psum | solution.py:70
  154.2 3.3 %fusion.4 = bf16[768,1280]{1,0:T(8,128)(2,1)} fusion(bf16[768,1280]{1,0:T(8,128)(2,1)S(1)} %copy-done, bf16[768,1280]{1,0:T(8,128)(2,1)} %all-reduce.2.cloned.1.call-done), kind=kLoop, calls=%fused_computation.7 | loop fusion | flops 3932160 | bytes 5898240 | tf_op jit(solution)/shard_map/convert_element_type | solution.py:71
  (4 shorter events, 0.1 us)
Async XLA Ops:
  6.5 34.6 %copy-start.5 = (f32[3,320]{1,0:T(4,128)S(1)}, f32[3,320]{1,0:T(4,128)}, u32[]{:S(2)}) copy-start(f32[3,320]{1,0:T(4,128)} %param.10) | copy-start | bytes 11524
  6.5 48.9 %all-gather.2.cloned.1.call-start = ((), (), s32[]{:S(2)}) async-start(), calls=%async_computation | async-start | bytes 3317760 | tf_op jit(solution)/shard_map/all_gather | solution.py:34
  7.3 146.9 %all-reduce.2.cloned.1.call-start = ((), (), s32[]{:S(2)}) async-start(), calls=%async_computation.1 | async-start | bytes 3932160 | tf_op jit(solution)/shard_map/psum | solution.py:70
  8.1 33.1 %collective-permute-start.2 = (s32[64]{0:T(128)S(1)}, s32[64]{0:T(128)S(1)}, u32[]{:S(2)}, u32[]{:S(2)}) collective-permute-start(s32[64]{0:T(128)S(1)} %get-tuple-element.14), channel_id=1, source_target_pairs={{0,4},{4,8},{8,12},{12,16},{16,20},{20,24},{24,28},{1,5},{5,9},{9,... | collective-permute-start | bytes 776 | tf_op jit(solution)/shard_map/ppermute | solution.py:18
  10.4 30.8 %collective-permute-start.3 = (s32[64]{0:T(128)S(1)}, s32[64]{0:T(128)S(1)}, u32[]{:S(2)}, u32[]{:S(2)}) collective-permute-start(s32[64]{0:T(128)S(1)} %get-tuple-element.13), channel_id=1, source_target_pairs={{4,0},{8,4},{12,8},{16,12},{20,16},{24,20},{28,24},{5,1},{9,5},{13... | collective-permute-start | bytes 776 | tf_op jit(solution)/shard_map/ppermute | solution.py:20
  41.4 19.4 %copy-start = (bf16[768,1280]{1,0:T(8,128)(2,1)S(1)}, bf16[768,1280]{1,0:T(8,128)(2,1)}, u32[]{:S(2)}) copy-start(bf16[768,1280]{1,0:T(8,128)(2,1)} %param.6) | copy-start | bytes 5898244
  41.4 19.4 %copy-start.6 = (f32[1280]{0:T(1024)S(1)}, f32[1280]{0:T(1024)}, u32[]{:S(2)}) copy-start(f32[1280]{0:T(1024)} %param.8) | copy-start | bytes 15364
  64.7 4.7 %copy-start.1 = (bf16[768,960]{0,1:T(8,128)(2,1)}, bf16[768,960]{0,1:T(8,128)(2,1)S(1)}, u32[]{:S(2)}) copy-start(bf16[768,960]{0,1:T(8,128)(2,1)S(1)} %add_convert_fusion) | copy-start | bytes 4423684
  65.6 6.5 %collective-permute-start = (bf16[64,640]{0,1:T(8,128)(2,1)}, bf16[64,640]{0,1:T(8,128)(2,1)}, u32[]{:S(2)}, u32[]{:S(2)}) collective-permute-start(bf16[64,640]{0,1:T(8,128)(2,1)} %get-tuple-element.8), channel_id=1, source_target_pairs={{0,4},{4,8},{8,12},{12,16},{16,20},{20,24},{24,28},{1,5},{5,9},{9,... | collective-permute-start | bytes 245768 | tf_op jit(solution)/shard_map/ppermute | solution.py:18
  69.4 8.6 %collective-permute-start.1 = (bf16[64,640]{0,1:T(8,128)(2,1)}, bf16[64,640]{0,1:T(8,128)(2,1)}, u32[]{:S(2)}, u32[]{:S(2)}) collective-permute-start(bf16[64,640]{0,1:T(8,128)(2,1)} %get-tuple-element.7), channel_id=1, source_target_pairs={{4,0},{8,4},{12,8},{16,12},{20,16},{24,20},{28,24},{5,1},{9,5},{13... | collective-permute-start | bytes 245768 | tf_op jit(solution)/shard_map/ppermute | solution.py:20
  78.0 1.4 copy-start.2
  79.3 0.9 copy-start.4
  82.0 1.2 copy-start.3
Sparse Core Ops, SparseCore 0:
  9.0 46.4 all-gather.1
  85.9 68.2 all-reduce.1
where the time goes:
time: 165 us; the launch traced here: 164 us
  waiting for transfers between devices  83.2 us (50%)
  blocking collectives  27.3 us (17%)
  local copies, waits for them, and re-layouts  13.7 us (8%)
  between operations  13.6 us (8%)
  other arithmetic  10.9 us (7%)
  starting transfers between devices  7.79 us (5%)
  matrix products  7.75 us (5%)
    psum x1, waiting for transfers between devices, local(): lax.psum(partial_out.astype(jnp.bfloat16), 'tensor').astype(jnp.float32)  68.4 us
    all_gather x1, blocking collectives, local(): lax.all_gather(w_out, ('section', 'dp'), axis=0, tiled=True)  27.3 us
    all_gather x1, waiting for transfers between devices, local(): piece = lax.all_gather(w_qkv, ('section', 'dp'), axis=0, tiled=True)  14.1 us
    all_gather x1, local copies, waits for them, and re-layouts, local(): piece = lax.all_gather(w_qkv, ('section', 'dp'), axis=0, tiled=True)  5.29 us
    unnamed x18, local copies, waits for them, and re-layouts  5.19 us
    ppermute x2, starting transfers between devices, with_halo(): lax.ppermute(tail, axis, [(i, (i + 1) % count) for i in range(ends)])  5.16 us
    dot_general x1, matrix products, local(): jnp.dot(normed, piece.reshape(count, 3 * local_cols), preferred_element_t...  3.88 us
  transfers between devices with their start and end apart: 6, of which 2 were waited for; matrix products, arithmetic and copies ran while one was open for 7% of the time, Pallas kernels for 0%

commit v1 on v0

--- a/solution.py
+++ b/solution.py
@@ -1,10 +1,16 @@
+import functools
+import math
+
 import jax
 import jax.numpy as jnp
 from jax import lax
+from jax.experimental import pallas as pl
+from jax.experimental.pallas import tpu as pltpu
 from jax.sharding import PartitionSpec as P
 
 HEAD = 80
 WIN = 64
+MESH = pl.DeviceIdType.MESH
 
 
 def with_halo(cells, sides, width):
@@ -71,6 +77,513 @@
     return (values_f + summed).astype(jnp.bfloat16)
 
 
+def flip(x):
+    return pltpu.roll(x.astype(jnp.float32), 64, 1).astype(x.dtype)
+
+
+def kernel(
+    sections,
+    x_ref, ids_ref, gain_ref, pack_ref, bias_ref, out_ref,
+    wp, normed, acc, q3, kv3, attn, wo, wof, idb, kid,
+    up_s, dn_s, sib_s, wp_r, wx_s, wy_s, wf_s, w_r, ws_s, ws_r,
+    id_s, id_r, h_s, h_r, ax_s, ay_s, af_s, a_r,
+):
+    rows, width = x_ref.shape
+    depth = width // (2 * sections)
+    halfd = depth // 2
+    wq_rows = 7 * depth + halfd
+    blocks = rows // 128
+    last = sections - 1
+    s, c, t = lax.axis_index("section"), lax.axis_index("dp"), lax.axis_index("tensor")
+    oc = 1 - c
+    tx = t + 1 - 2 * (t % 2)
+    ty = (t + 2) % 4
+    td = (tx + 2) % 4
+    up, dn, sib = (s + 1, c, t), (s - 1, c, t), (s, oc, t)
+    xn, yn = (s, c, tx), (s, c, ty)
+    hz = s - 1 + 2 * c
+    hdev = (hz, oc, t)
+    has_up, has_dn = s < last, s > 0
+    has_h = jnp.logical_and(hz >= 0, hz <= last)
+
+    def rc(src, dst, ss, rs, dev):
+        return pltpu.make_async_remote_copy(
+            src_ref=src, dst_ref=dst, send_sem=ss, recv_sem=rs, device_id=dev, device_id_type=MESH
+        )
+
+    barrier = pltpu.get_barrier_semaphore()
+
+    def greet(dev):
+        pl.semaphore_signal(barrier, inc=1, device_id=dev, device_id_type=MESH)
+
+    greet(sib)
+    greet(xn)
+    greet(yn)
+
+    @pl.when(has_up)
+    def _():
+        greet(up)
+
+    @pl.when(has_dn)
+    def _():
+        greet(dn)
+
+    @pl.when(has_h)
+    def _():
+        greet(hdev)
+
+    peers = 3 + has_up.astype(jnp.int32) + has_dn.astype(jnp.int32) + has_h.astype(jnp.int32)
+    pl.semaphore_wait(barrier, peers)
+
+    def src_of(j, own):
+        return pack_ref if own else wp.at[2 * j + c]
+
+    def d_up(j, own=False):
+        return rc(src_of(j, own), wp.at[2 * j + c], up_s.at[j], wp_r.at[2 * j + c], up)
+
+    def d_dn(j, own=False):
+        return rc(src_of(j, own), wp.at[2 * j + c], dn_s.at[j], wp_r.at[2 * j + c], dn)
+
+    def d_sib(j, own=False):
+        return rc(src_of(j, own), wp.at[2 * j + c], sib_s.at[j], wp_r.at[2 * j + c], sib)
+
+    def got(j, parity):
+        g = 2 * j + parity
+        rc(wp.at[g], wp.at[g], sib_s.at[j], wp_r.at[g], sib).wait_recv()
+
+    def wo_src(j, own):
+        return src_of(j, own).at[pl.ds(wq_rows, 2 * depth + halfd)]
+
+    def d_wx(j, own=False):
+        return rc(wo_src(j, own), wo.at[c, 0, j], wx_s.at[j], w_r.at[0, j], xn)
+
+    def d_wy(j, own=False):
+        return rc(wo_src(j, own), wo.at[c, 1, j], wy_s.at[j], w_r.at[1, j], yn)
+
+    def d_fx(j):
+        return rc(wo.at[c, 0, j], wo.at[c, 2, j], wf_s.at[j], w_r.at[2, j], yn)
+
+    def d_fy(j):
+        return rc(wo.at[c, 1, j], wo.at[c, 2, j], wf_s.at[j], w_r.at[2, j], xn)
+
+    def d_ws():
+        return rc(wo.at[c], wo.at[c], ws_s, ws_r, sib)
+
+    d_wos = (d_wx, d_wy)
+
+    @pl.when(has_up)
+    def _():
+        d_up(s, True).start()
+
+    @pl.when(has_dn)
+    def _():
+        d_dn(s, True).start()
+
+    d_sib(s, True).start()
+    for d in d_wos:
+        d(s, True).start()
+
+    def d_id(k):
+        return functools.partial(rc, ids_ref, idb.at[2 - 2 * k], id_s.at[k], id_r.at[1 - k])
+
+    @pl.when(c == 0)
+    def _():
+        d_id(1)(sib).start()
+
+        @pl.when(has_h)
+        def _():
+            d_id(0)(hdev).start()
+
+    @pl.when(c == 1)
+    def _():
+        d_id(0)(sib).start()
+
+        @pl.when(has_h)
+        def _():
+            d_id(1)(hdev).start()
+
+    def norm_block(i, _):
+        r = pl.ds(pl.multiple_of(i * 128, 128), 128)
+        v = x_ref[r, :].astype(jnp.float32)
+        sc = lax.rsqrt(jnp.mean(v * v, axis=-1, keepdims=True) + 1e-06)
+        n = v * sc * gain_ref[...]
+        for g in range(2 * sections):
+            normed[g, r, :] = n[:, g * depth : (g + 1) * depth].astype(jnp.bfloat16)
+        acc[r, :] = jnp.broadcast_to(bias_ref[...], (128, 1024))
+        return 0
+
+    lax.fori_loop(0, blocks, norm_block, 0)
+
+    def mm(ref, g):
+        a = normed[g]
+        for p in range(4):
+            lo = ref[pl.ds(2 * p * depth, depth), :]
+            if p < 3:
+                hi = ref[pl.ds((2 * p + 1) * depth, depth), :]
+            else:
+                h = ref[pl.ds(7 * depth, halfd), :]
+                hi = jnp.concatenate([h, flip(h)], axis=0)
+            w = jnp.concatenate([lo, hi], axis=1)
+            acc[:, 256 * p : 256 * p + 256] += jnp.dot(a, w, preferred_element_type=jnp.float32)
+
+    def spread(j):
+        rc(wo.at[c, 0, j], wo.at[c, 0, j], wx_s.at[j], w_r.at[0, j], xn).wait_recv()
+        rc(wo.at[c, 1, j], wo.at[c, 1, j], wy_s.at[j], w_r.at[1, j], yn).wait_recv()
+
+        @pl.when(j % 2 == 0)
+        def _():
+            d_fx(j).start()
+
+        @pl.when(j % 2 == 1)
+        def _():
+            d_fy(j).start()
+
+    mm(pack_ref, 2 * s + c)
+    got(s, oc)
+    mm(wp.at[2 * s + oc], 2 * s + oc)
+    spread(s)
+
+    def step(d, _):
+        jb, ja = s - d, s + d
+
+        @pl.when(jb >= 0)
+        def _():
+            got(jb, c)
+
+            @pl.when(has_up)
+            def _():
+                d_up(jb).start()
+
+            d_sib(jb).start()
+            for e in d_wos:
+                e(jb).start()
+
+        @pl.when(ja <= last)
+        def _():
+            got(ja, c)
+
+            @pl.when(has_dn)
+            def _():
+                d_dn(ja).start()
+
+            d_sib(ja).start()
+            for e in d_wos:
+                e(ja).start()
+
+        for k in range(2):
+            j = s - d + 2 * d * k
+
+            @pl.when(jnp.logical_and(j >= 0, j <= last))
+            def _():
+                def core(m, _):
+                    g = 2 * j + lax.rem(c + m, 2)
+
+                    @pl.when(m == 1)
+                    def _():
+                        got(j, oc)
+
+                    mm(wp.at[g], g)
+                    return 0
+
+                lax.fori_loop(0, 2, core, 0)
+                spread(j)
+
+        return 0
+
+    lax.fori_loop(1, sections, step, 0)
+
+    def settle(i, _):
+        r = pl.ds(pl.multiple_of(i * 128, 128), 128)
+        rk = pl.ds(pl.multiple_of(i * 128 + WIN, WIN), 128)
+        p = acc[r, :].astype(jnp.bfloat16)
+        q3[r, 0:256] = p[:, 0:256]
+        q3[r, 256:384] = p[:, 768:896]
+        kv3[rk, 0:256] = p[:, 256:512]
+        kv3[rk, 256:384] = p[:, 896:1024]
+        kv3[rk, 384:640] = p[:, 512:768]
+        kv3[rk, 640:768] = p[:, 768:896]
+        return 0
+
+    lax.fori_loop(0, blocks, settle, 0)
+
+    def d_h(k):
+        src = kv3.at[pl.ds(WIN if k == 0 else rows, WIN)]
+        dst = kv3.at[pl.ds(rows + WIN if k == 0 else 0, WIN)]
+        return functools.partial(rc, src, dst, h_s.at[k], h_r.at[1 - k])
+
+    @pl.when(c == 0)
+    def _():
+        d_h(1)(sib).start()
+
+        @pl.when(has_h)
+        def _():
+            d_h(0)(hdev).start()
+
+        @pl.when(jnp.logical_not(has_h))
+        def _():
+            kv3[0:WIN, :] = jnp.zeros((WIN, 768), jnp.bfloat16)
+            idb[0] = jnp.full((8, 128), -1, jnp.int32)
+
+    @pl.when(c == 1)
+    def _():
+        d_h(0)(sib).start()
+
+        @pl.when(has_h)
+        def _():
+            d_h(1)(hdev).start()
+
+        @pl.when(jnp.logical_not(has_h))
+        def _():
+            kv3[rows + WIN : rows + 2 * WIN, :] = jnp.zeros((WIN, 768), jnp.bfloat16)
+            idb[2] = jnp.full((8, 128), -1, jnp.int32)
+
+    def wait_side(d, k):
+        @pl.when(jnp.logical_or(c == 1 - k, has_h))
+        def _():
+            d(1 - k)(sib).wait_recv()
+
+    wait_side(d_id, 0)
+    wait_side(d_id, 1)
+    chain = jnp.concatenate([idb[0, blocks - 1 : blocks], ids_ref[0:blocks, :], idb[2, 0:1]], axis=0)
+    lane8 = lax.broadcasted_iota(jnp.int32, (8, 128), 1)
+    after = jnp.concatenate([chain[1:], chain[:1]], axis=0)
+    kid[...] = pltpu.roll(jnp.where(lane8 < 64, after, chain), 64, 1)
+
+    lane = lax.broadcasted_iota(jnp.int32, (128, 128), 1)
+    scale = math.log2(math.e) / HEAD**0.5
+    zero = jnp.zeros((128, 128), jnp.bfloat16)
+
+    def d_ax(b):
+        r = pl.ds(pl.multiple_of(b * 128, 128), 128)
+        return rc(attn.at[t, r], attn.at[t, r], ax_s.at[b], a_r.at[0, b], xn)
+
+    def d_ay(b):
+        r = pl.ds(pl.multiple_of(b * 128, 128), 128)
+        return rc(attn.at[t, r], attn.at[t, r], ay_s.at[b], a_r.at[1, b], yn)
+
+    def d_afx(b):
+        r = pl.ds(pl.multiple_of(b * 128, 128), 128)
+        return rc(attn.at[tx, r], attn.at[tx, r], af_s.at[b], a_r.at[2, b], yn)
+
+    def d_afy(b):
+        r = pl.ds(pl.multiple_of(b * 128, 128), 128)
+        return rc(attn.at[ty, r], attn.at[ty, r], af_s.at[b], a_r.at[2, b], xn)
+
+    def attend(b):
+        r = pl.ds(pl.multiple_of(b * 128, 128), 128)
+        rk = pl.ds(pl.multiple_of(b * 128, 128), 256)
+        idq = jnp.transpose(jnp.broadcast_to(ids_ref[pl.ds(b, 1), :], (128, 128)))
+        ok = jnp.concatenate([idq == kid[pl.ds(b, 1), :], idq == kid[pl.ds(b + 1, 1), :]], axis=1)
+        qa, qb, qh = q3[r, 0:128], q3[r, 128:256], q3[r, 256:384]
+        parts = (
+            (jnp.where(lane < 80, qa, zero), 0, 128),
+            (
+                jnp.concatenate(
+                    [jnp.where(lane >= 80, qa, zero), jnp.where(lane < 32, qb, zero)], axis=1
+                ),
+                0,
+                256,
+            ),
+            (jnp.where(jnp.logical_and(lane >= 32, lane < 112), qb, zero), 128, 256),
+            (
+                jnp.concatenate(
+                    [jnp.where(lane >= 112, qb, zero), jnp.where(lane < 64, qh, zero)], axis=1
+                ),
+                128,
+                384,
+            ),
+        )
+        outs = []
+        for q, lo, hi in parts:
+            sc = lax.dot_general(
+                q, kv3[rk, lo:hi], (((1,), (1,)), ((), ())), preferred_element_type=jnp.float32
+            )
+            sc = jnp.where(ok, sc, jnp.float32(-1e30))
+            top = jnp.max(sc, axis=-1, keepdims=True)
+            e = jnp.exp2((sc - top) * scale)
+            total = jnp.sum(e, axis=-1, keepdims=True)
+            o = jnp.dot(
+                e.astype(jnp.bfloat16), kv3[rk, 384 + lo : 384 + hi], preferred_element_type=jnp.float32
+            )
+            outs.append(o * (1.0 / total))
+        o0, o1, o2, o3 = outs
+        attn[t, r, 0:128] = jnp.where(lane < 80, o0, o1[:, :128]).astype(jnp.bfloat16)
+        attn[t, r, 128:256] = jnp.where(
+            lane < 32, o1[:, 128:], jnp.where(lane < 112, o2, o3[:, :128])
+        ).astype(jnp.bfloat16)
+        attn[t, r, 256:384] = jnp.where(lane >= 64, o3[:, 128:], jnp.float32(0.0)).astype(jnp.bfloat16)
+        d_ax(b).start()
+        d_ay(b).start()
+
+    def relay(b):
+        r = pl.ds(pl.multiple_of(b * 128, 128), 128)
+        rc(attn.at[tx, r], attn.at[tx, r], ax_s.at[b], a_r.at[0, b], xn).wait_recv()
+        rc(attn.at[ty, r], attn.at[ty, r], ay_s.at[b], a_r.at[1, b], yn).wait_recv()
+
+        @pl.when(b % 2 == 0)
+        def _():
+            d_afx(b).start()
+
+        @pl.when(b % 2 == 1)
+        def _():
+            d_afy(b).start()
+
+    def order(i):
+        return jnp.where(i < blocks - 2, i + 1, jnp.where(i == blocks - 2, 0, blocks - 1))
+
+    def attend_step(i, _):
+        @pl.when(i == blocks - 2)
+        def _():
+            wait_side(d_h, 0)
+            wait_side(d_h, 1)
+
+        attend(order(i))
+
+        @pl.when(i == 2)
+        def _():
+            def diag(j, _):
+                rc(wo.at[c, 2, j], wo.at[c, 2, j], wf_s.at[j], w_r.at[2, j], xn).wait_recv()
+                return 0
+
+            lax.fori_loop(0, sections, diag, 0)
+            d_ws().start()
+
+        @pl.when(i >= 2)
+        def _():
+            relay(order(i - 2))
+
+        return 0
+
+    lax.fori_loop(0, blocks, attend_step, 0)
+
+    rc(wo.at[oc], wo.at[oc], ws_s, ws_r, sib).wait_recv()
+
+    def unpack(src, tt, g):
+        base = g * depth
+        wof[tt, pl.ds(pl.multiple_of(base, 16), depth), 0:128] = src[0:depth, :]
+        wof[tt, pl.ds(pl.multiple_of(base, 16), depth), 128:256] = src[depth : 2 * depth, :]
+        h = src[2 * depth : 2 * depth + halfd, :]
+        wof[tt, pl.ds(pl.multiple_of(base, 16), halfd), 256:384] = flip(h)
+        wof[tt, pl.ds(pl.multiple_of(base + halfd, 16), halfd), 256:384] = h
+
+    def unpack_all(j, _):
+        for m in range(2):
+            g = 2 * j + m
+            for k, tt in enumerate((tx, ty, td)):
+                unpack(wo.at[m, k, j], tt, g)
+
+            @pl.when(g != 2 * s + c)
+            def _():
+                unpack(wp.at[g, pl.ds(wq_rows, 2 * depth + halfd)], t, g)
+
+        return 0
+
+    lax.fori_loop(0, sections, unpack_all, 0)
+    unpack(pack_ref.at[pl.ds(wq_rows, 2 * depth + halfd)], t, 2 * s + c)
+
+    def project(i, _):
+        @pl.when(i < 2)
+        def _():
+            relay(order(i + blocks - 2))
+
+        b = order(i)
+        r = pl.ds(pl.multiple_of(b * 128, 128), 128)
+        rc(attn.at[td, r], attn.at[td, r], af_s.at[b], a_r.at[2, b], xn).wait_recv()
+        a = jnp.concatenate([attn[k, r, :] for k in range(4)], axis=1)
+        for n in range(width // 256):
+            w = jnp.concatenate([wof[k, 256 * n : 256 * n + 256, :] for k in range(4)], axis=1)
+            total = lax.dot_general(
+                a, w, (((1,), (1,)), ((), ())), preferred_element_type=jnp.float32
+            )
+            cols = slice(256 * n, 256 * n + 256)
+            out_ref[r, cols] = (x_ref[r, cols].astype(jnp.float32) + total).astype(jnp.bfloat16)
+        return 0
+
+    lax.fori_loop(0, blocks, project, 0)
+
+    def sent_w(j, _):
+        @pl.when(jnp.logical_and(has_up, j <= s))
+        def _():
+            d_up(j).wait_send()
+
+        @pl.when(jnp.logical_and(has_dn, j >= s))
+        def _():
+            d_dn(j).wait_send()
+
+        d_sib(j).wait_send()
+        d_wx(j).wait_send()
+        d_wy(j).wait_send()
+        d_fx(j).wait_send()
+        return 0
+
+    lax.fori_loop(0, sections, sent_w, 0)
+    d_ws().wait_send()
+
+    def sent_a(b, _):
+        d_ax(b).wait_send()
+        d_ay(b).wait_send()
+        d_afx(b).wait_send()
+        return 0
+
+    lax.fori_loop(0, blocks, sent_a, 0)
+    for d in (d_id, d_h):
+        for k in range(2):
+
+            @pl.when(jnp.logical_or(c == 1 - k, has_h))
+            def _():
+                d(k)(sib).wait_send()
+
+
+def fold(w):
+    half = w.shape[0] // 2
+    return jnp.concatenate([w[:half], w[half:]], axis=1)
+
+
+def fused(sections, patches, window_ids, norm_gain, w_qkv, qkv_bias, w_out):
+    rows, width = patches.shape
+    depth = w_qkv.shape[0]
+    blocks = rows // 128
+    q, k, v = w_qkv[:, 0], w_qkv[:, 1], w_qkv[:, 2]
+    tiles = [w[:, lo : lo + 128] for w in (q, k, v) for lo in (0, 128)]
+    tiles += [jnp.concatenate([q[:, 256:], v[:, 256:]], axis=1), fold(k[:, 256:])]
+    tiles += [w_out[:, :128], w_out[:, 128:256], fold(w_out[:, 256:])]
+    pack = jnp.concatenate(tiles, axis=0)
+    b = qkv_bias
+    bias = jnp.concatenate(
+        [b[0, :256], b[1, :256], b[2, :256], b[0, 256:], b[2, 256:], b[1, 256:], jnp.zeros((64,), b.dtype)]
+    )[None]
+    ids = jnp.pad(window_ids.reshape(blocks, 128), ((0, 8 - blocks), (0, 0)))
+    bf, dma = jnp.bfloat16, pltpu.SemaphoreType.DMA
+    shards = 2 * sections
+    wo_rows = 2 * depth + depth // 2
+    vmem = pl.BlockSpec(memory_space=pltpu.VMEM)
+    return pl.pallas_call(
+        functools.partial(kernel, sections),
+        out_shape=jax.ShapeDtypeStruct((rows, width), bf),
+        in_specs=[vmem] * 5,
+        out_specs=vmem,
+        scratch_shapes=[
+            pltpu.VMEM((shards, 10 * depth, 128), bf),
+            pltpu.VMEM((shards, rows, depth), bf),
+            pltpu.VMEM((rows, 1024), jnp.float32),
+            pltpu.VMEM((rows, 384), bf),
+            pltpu.VMEM((rows + 2 * WIN, 768), bf),
+            pltpu.VMEM((4, rows, 384), bf),
+            pltpu.VMEM((2, 3, sections, wo_rows, 128), bf),
+            pltpu.VMEM((4, width, 384), bf),
+            pltpu.VMEM((3, 8, 128), jnp.int32),
+            pltpu.VMEM((8, 128), jnp.int32),
+            dma((sections,)), dma((sections,)), dma((sections,)), dma((shards,)),
+            dma((sections,)), dma((sections,)), dma((sections,)), dma((3, sections)), dma, dma,
+            dma((2,)), dma((2,)), dma((2,)), dma((2,)),
+            dma((blocks,)), dma((blocks,)), dma((blocks,)), dma((3, blocks)),
+        ],
+        compiler_params=pltpu.CompilerParams(
+            collective_id=0, has_side_effects=True, vmem_limit_bytes=52 * 1024 * 1024
+        ),
+    )(patches, ids, norm_gain[None], pack, bias)
+
+
 def solution(mesh):
     placed = (
         P(("section", "dp"), None),
@@ -80,6 +593,23 @@
         P(None, "tensor"),
         P(("section", "dp"), "tensor"),
     )
+    sections, cores, heads = mesh.shape["section"], mesh.shape["dp"], mesh.shape["tensor"]
+
+    def body(*args):
+        patches, w_qkv = args[0], args[3]
+        rows, width = patches.shape
+        depth = w_qkv.shape[0]
+        fits = (
+            cores == 2
+            and heads == 4
+            and sections % 2 == 0
+            and depth % 32 == 0
+            and w_qkv.shape[2] == 320
+            and width % 256 == 0
+            and rows == 768
+        )
+        return fused(sections, *args) if fits else local(*args)
+
     return jax.shard_map(
-        local, mesh=mesh, in_specs=placed, out_specs=P(("section", "dp"), None), check_vma=False
+        body, mesh=mesh, in_specs=placed, out_specs=P(("section", "dp"), None), check_vma=False
     )

time: 165 us -> 79.9 us (0.48)
  waiting for transfers between devices: 83.2 us -> 0 us
  Pallas kernels: 0 us -> 69.6 us
  blocking collectives: 27.3 us -> 0 us
  between operations: 13.6 us -> 0.08 us
  other arithmetic: 10.9 us -> 0.28 us
  starting transfers between devices: 7.79 us -> 0 us
  matrix products: 7.75 us -> 0 us
  local copies, waits for them, and re-layouts: 13.7 us -> 9.48 us
    pallas_call x0 -> x1, Pallas kernels: none -> 69.6 us  [fused(): pl.pallas_call(functools.partial(kernel, sections), out_shape=jax.ShapeDt...]
    psum x1 -> x0, waiting for transfers between devices: 68.4 us -> none  [local(): lax.psum(partial_out.astype(jnp.bfloat16), 'tensor').astype(jnp.float32)]
    all_gather x1 -> x0, blocking collectives: 27.3 us -> none  [local(): lax.all_gather(w_out, ('section', 'dp'), axis=0, tiled=True)]
    all_gather x1 -> x0, waiting for transfers between devices: 14.1 us -> none  [local(): piece = lax.all_gather(w_qkv, ('section', 'dp'), axis=0, tiled=True)]
    dot_general x4 -> x0, matrix products: 7.75 us -> none  [the longest x1 3.88 us: local(): jnp.dot(normed, piece.reshape(count, 3 * local_cols), preferred_element_t...]
    ppermute x4 -> x0, starting transfers between devices: 7.75 us -> none  [the longest x2 5.16 us: with_halo(): lax.ppermute(tail, axis, [(i, (i + 1) % count) for i in range(ends)])]
    all_gather x1 -> x0, local copies, waits for them, and re-layouts: 5.29 us -> none  [local(): piece = lax.all_gather(w_qkv, ('section', 'dp'), axis=0, tiled=True)]
    convert_element_type x1 -> x0, other arithmetic: 3.28 us -> none  [local(): return (values_f + summed).astype(jnp.bfloat16)]
  transfers between devices with their start and end apart: 6 -> 0, of which waited for: 2 -> 0; matrix products, arithmetic and copies ran while one was open for 7% -> 0% of each run, Pallas kernels for 0% -> 0%
where the time goes in v1:
time: 79.9 us; the launch traced here: 79.4 us
  Pallas kernels  69.6 us (87%)
  local copies, waits for them, and re-layouts  9.48 us (12%)
    pallas_call x1, Pallas kernels, fused(): pl.pallas_call(functools.partial(kernel, sections), out_shape=jax.ShapeDt...  69.6 us
    unnamed x9, local copies, waits for them, and re-layouts  4.6 us

profile of v1, /device:TPU:0, one launch (start us, length us, event | category | flops | bytes accessed | tf_op | source)
XLA Modules:
  0.0 79.4 jit_solution(1314147980862220659)
XLA Ops:
  0.0 0.8 %slice_bitcast_fusion.3 = (f32[64]{0:T(128)S(1)}, f32[64]{0:T(128)S(1)}, f32[64]{0:T(128)S(1)}) fusion(f32[3,320]{1,0:T(4,128)} %param.10), kind=kLoop, calls=%fused_computation.14 | loop fusion | bytes 1536 | tf_op jit(solution)/shard_map/squeeze | solution.py:553
  0.8 0.8 %fusion.2 = (f32[1,256]{1,0:T(1,128)S(1)}, f32[1,256]{1,0:T(1,128)S(1)}, f32[1,256]{1,0:T(1,128)S(1)}) fusion(f32[3,320]{1,0:T(4,128)} %param.10), kind=kLoop, calls=%fused_computation.19 | loop fusion | bytes 6144 | tf_op jit(solution)/shard_map/slice | solution.py:553
  1.6 0.1 concatenate.19
  1.7 0.7 pad.4.ids_ref
  2.4 0.7 broadcast_in_dim.9.gain_ref
  3.1 0.7 fusion
  3.8 1.1 %slice_bitcast_fusion = (bf16[160,320]{1,0:T(8,128)(2,1)S(1)}, bf16[160,320]{1,0:T(8,128)(2,1)S(1)}, bf16[160,320]{1,0:T(8,128)(2,1)S(1)}) fusion(bf16[160,3,320]{2,0,1:T(8,128)(2,1)} %param.9), kind=kLoop, calls=%fused_computation | loop fusion | bytes 614400 | tf_op jit(solution)/shard_map/squeeze | solution.py:546
  5.0 0.1 maximum_dynamic-update-slice_fusion
  5.1 0.1 constant_dynamic-update-slice_fusion.1
  5.2 0.8 %slice_dynamic-update-slice_fusion.7 = bf16[1600,128]{1,0:T(8,128)(2,1)S(1)} fusion(bf16[1600,128]{1,0:T(8,128)(2,1)S(1)} %constant_dynamic-update-slice_fusion.1, bf16[160,320]{1,0:T(8,128)(2,1)} %param.11), kind=kLoop, calls=%fused_computation.11 | loop fusion | bytes 81920
  6.0 0.8 slice_dynamic-update-slice_fusion.6
  6.8 0.1 constant_dynamic-update-slice_fusion.pack_ref
  6.9 69.6 %shard_map.64 = bf16[768,1280]{1,0:T(8,128)(2,1)} custom-call(bf16[768,1280]{1,0:T(8,128)(2,1)} %x_ref.1, s32[8,128]{1,0:T(8,128)S(1)} %pad.4.ids_ref, f32[1,1280]{1,0:T(1,128)S(1)} %broadcast_in_dim.9.gain_ref, bf16[1600,128]{1,0:T(8,128)(2,1)S(1)} %constant_dynamic-update-slice_fusion.pack_ref, f32[1,1024]{1,0:T(1,128)S(1)} %bitcast.17), custom_call_target="tpu_custom_call" | custom-call | tf_op jit(solution)/shard_map/pallas_call | solution.py:560
  76.5 2.9 %copy.18 = bf16[768,1280]{1,0:T(8,128)(2,1)} copy(bf16[768,1280]{1,0:T(8,128)(2,1)} %shard_map.64) | data formatting | bytes 3932160
  (10 shorter events, 0.1 us)

commit v2 on v0

--- a/solution.py
+++ b/solution.py
@@ -1,10 +1,16 @@
+import functools
+import math
+
 import jax
 import jax.numpy as jnp
 from jax import lax
+from jax.experimental import pallas as pl
+from jax.experimental.pallas import tpu as pltpu
 from jax.sharding import PartitionSpec as P
 
 HEAD = 80
 WIN = 64
+MESH = pl.DeviceIdType.MESH
 
 
 def with_halo(cells, sides, width):
@@ -71,6 +77,611 @@
     return (values_f + summed).astype(jnp.bfloat16)
 
 
+def rot(x, by):
+    return pltpu.roll(x.astype(jnp.float32), by, 1).astype(x.dtype)
+
+
+def kernel(
+    sections,
+    x_ref, ids_ref, gain_ref, w_ref, wout_ref, bias_ref, out_ref,
+    tmp, tmpb, pk, bias, wp, normed, acc, q3, kv3, rbuf, at0, at1, wo, wof, idb, kid,
+    up_s, dn_s, sib_s, wp_r, wx_s, wy_s, wf_s, w_r, ws_s, ws_r,
+    id_s, id_r, h_s, h_r, ax_s, ay_s, af_s, a_r,
+):
+    rows, width = x_ref.shape
+    depth = width // (2 * sections)
+    halfd = depth // 2
+    region = ((0, 4 * depth), (4 * depth, 2 * depth + halfd), (6 * depth + halfd, 4 * depth))
+    half_at = (0, 2)
+    blocks = rows // 128
+    last = sections - 1
+    bf = jnp.bfloat16
+    s, c, t = lax.axis_index("section"), lax.axis_index("dp"), lax.axis_index("tensor")
+    oc = 1 - c
+    tx = t + 1 - 2 * (t % 2)
+    ty = (t + 2) % 4
+    td = (tx + 2) % 4
+    up, dn, sib = (s + 1, c, t), (s - 1, c, t), (s, oc, t)
+    xn, yn = (s, c, tx), (s, c, ty)
+    hz = s - 1 + 2 * c
+    hdev = (hz, oc, t)
+    has_up, has_dn = s < last, s > 0
+    has_h = jnp.logical_and(hz >= 0, hz <= last)
+
+    def rc(src, dst, ss, rs, dev):
+        return pltpu.make_async_remote_copy(
+            src_ref=src, dst_ref=dst, send_sem=ss, recv_sem=rs, device_id=dev, device_id_type=MESH
+        )
+
+    barrier = pltpu.get_barrier_semaphore()
+
+    def greet(dev):
+        pl.semaphore_signal(barrier, inc=1, device_id=dev, device_id_type=MESH)
+
+    greet(sib)
+    greet(xn)
+    greet(yn)
+
+    @pl.when(has_up)
+    def _():
+        greet(up)
+
+    @pl.when(has_dn)
+    def _():
+        greet(dn)
+
+    @pl.when(has_h)
+    def _():
+        greet(hdev)
+
+    def lanes(n):
+        return lax.broadcasted_iota(jnp.int32, (n, 128), 1)
+
+    def arrange(h, q, k, v):
+        n = q[0].shape[0]
+        la = lanes(n)
+        if h == 0:
+            main = [z[0] for z in (q, k, v)]
+            rest = (q[1], rot(k[1], 32), rot(v[1], 64))
+        else:
+            main = [jnp.where(la < 32, z[2], z[1]) for z in (q, k, v)]
+            rest = (rot(q[2], 96), k[2], rot(v[2], 32))
+        more = jnp.where(la < 32, rest[0], jnp.where(la < 64, rest[1], rest[2]))
+        return main + [jnp.where(la < 96, more, jnp.zeros_like(more))]
+
+    def tiles(ref, i):
+        return [ref[i, :, 128 * m : 128 * m + 128] for m in range(3)]
+
+    for i in range(3):
+        tmp[i, :, 256:384] = jnp.zeros((depth, 128), bf)
+        tmp[i, :, 0:320] = w_ref[i]
+    tmp[3, :, 256:384] = jnp.zeros((depth, 128), bf)
+    tmp[3, :, 0:320] = wout_ref[...]
+    qkv = [tiles(tmp, i) for i in range(3)]
+    for h in range(2):
+        for m, tile in enumerate(arrange(h, *qkv)):
+            base = region[half_at[h]][0] + m * depth
+            pk[base : base + depth, :] = tile
+    w0, w1, w2 = tiles(tmp, 3)
+    la = lanes(depth)
+    base = region[1][0]
+    pk[base : base + depth, :] = w0
+    pk[base + depth : base + 2 * depth, :] = jnp.where(la < 32, w2, w1)
+    wr = rot(jnp.where(la < 32, w1, w2), 64)
+    pk[base + 2 * depth : base + 2 * depth + halfd, :] = jnp.where(
+        lanes(halfd) < 64, rot(wr[:halfd], 64), wr[halfd:]
+    )
+    idb[1] = jnp.zeros((8, 128), jnp.int32)
+    idb[1, 0:blocks, :] = ids_ref[...]
+
+    peers = 3 + has_up.astype(jnp.int32) + has_dn.astype(jnp.int32) + has_h.astype(jnp.int32)
+    pl.semaphore_wait(barrier, peers)
+
+    def src_of(k, j, own):
+        r = pl.ds(*region[k])
+        return pk.at[r] if own else wp.at[2 * j + c, r]
+
+    def d_z(sem, dev, k, j, own):
+        g = 2 * j + c
+        return rc(src_of(k, j, own), wp.at[g, pl.ds(*region[k])], sem.at[k, j], wp_r.at[k, g], dev)
+
+    def d_up(k, j, own=False):
+        return d_z(up_s, up, k, j, own)
+
+    def d_dn(k, j, own=False):
+        return d_z(dn_s, dn, k, j, own)
+
+    def d_sib(k, j, own=False):
+        return d_z(sib_s, sib, k, j, own)
+
+    def got(k, j, parity):
+        v = wp.at[2 * j + parity, pl.ds(*region[k])]
+        rc(v, v, sib_s.at[k, j], wp_r.at[k, 2 * j + parity], sib).wait_recv()
+
+    def d_wx(j, own=False):
+        return rc(src_of(1, j, own), wo.at[c, 0, j], wx_s.at[j], w_r.at[0, j], xn)
+
+    def d_wy(j, own=False):
+        return rc(src_of(1, j, own), wo.at[c, 1, j], wy_s.at[j], w_r.at[1, j], yn)
+
+    def d_fx(j):
+        return rc(wo.at[c, 0, j], wo.at[c, 2, j], wf_s.at[j], w_r.at[2, j], yn)
+
+    def d_fy(j):
+        return rc(wo.at[c, 1, j], wo.at[c, 2, j], wf_s.at[j], w_r.at[2, j], xn)
+
+    def d_ws():
+        return rc(wo.at[c], wo.at[c], ws_s, ws_r, sib)
+
+    def start_own(k):
+        @pl.when(has_up)
+        def _():
+            d_up(k, s, True).start()
+
+        @pl.when(has_dn)
+        def _():
+            d_dn(k, s, True).start()
+
+        d_sib(k, s, True).start()
+        if k == 1:
+            d_wx(s, True).start()
+            d_wy(s, True).start()
+
+    def pass_on(k, d):
+        jb, ja = s - d, s + d
+
+        @pl.when(jb >= 0)
+        def _():
+            got(k, jb, c)
+
+            @pl.when(has_up)
+            def _():
+                d_up(k, jb).start()
+
+            d_sib(k, jb).start()
+            if k == 1:
+                d_wx(jb).start()
+                d_wy(jb).start()
+
+        @pl.when(ja <= last)
+        def _():
+            got(k, ja, c)
+
+            @pl.when(has_dn)
+            def _():
+                d_dn(k, ja).start()
+
+            d_sib(k, ja).start()
+            if k == 1:
+                d_wx(ja).start()
+                d_wy(ja).start()
+
+    start_own(0)
+    start_own(1)
+
+    def d_id(k):
+        return functools.partial(rc, idb.at[1], idb.at[2 - 2 * k], id_s.at[k], id_r.at[1 - k])
+
+    def to_sides(d):
+        for k in range(2):
+
+            @pl.when(c == 1 - k)
+            def _():
+                d(k)(sib).start()
+
+            @pl.when(jnp.logical_and(c == k, has_h))
+            def _():
+                d(k)(hdev).start()
+
+    to_sides(d_id)
+
+    tmpb[:, 256:384] = jnp.zeros((8, 128), jnp.float32)
+    tmpb[0:3, 0:320] = bias_ref[...]
+    bt = [
+        [jnp.broadcast_to(tmpb[i : i + 1, 128 * m : 128 * m + 128], (8, 128)) for m in range(3)]
+        for i in range(3)
+    ]
+    for h in range(2):
+        bias[h] = jnp.concatenate(arrange(h, *bt), axis=1)
+
+    gain = jnp.concatenate([gain_ref[i : i + 1, :] for i in range(width // 128)], axis=1)
+
+    def norm_block(i, _):
+        r = pl.ds(pl.multiple_of(i * 128, 128), 128)
+        v = x_ref[r, :].astype(jnp.float32)
+        sc = lax.rsqrt(jnp.mean(v * v, axis=-1, keepdims=True) + 1e-06)
+        n = v * sc * gain
+        for g in range(2 * sections):
+            normed[g, r, :] = n[:, g * depth : (g + 1) * depth].astype(bf)
+        return 0
+
+    lax.fori_loop(0, blocks, norm_block, 0)
+
+    def mm(h, ref, g):
+        a = normed[g]
+        base = region[half_at[h]][0]
+        for p in range(2):
+            lo = ref[pl.ds(base + 2 * p * depth, depth), :]
+            hi = ref[pl.ds(base + (2 * p + 1) * depth, depth), :]
+            w = jnp.concatenate([lo, hi], axis=1)
+            acc[:, 256 * p : 256 * p + 256] += jnp.dot(a, w, preferred_element_type=jnp.float32)
+
+    def mm_own(h):
+        acc[...] = jnp.broadcast_to(bias[h, 0:1, :], (rows, 512))
+        mm(h, pk, 2 * s + c)
+        got(half_at[h], s, oc)
+        mm(h, wp.at[2 * s + oc], 2 * s + oc)
+
+    def mm_far(h, d):
+        def one(n, _):
+            j = jnp.where(n % 2 == 0, s - d, s + d)
+            parity = jnp.where(n < 2, c, oc)
+
+            @pl.when(jnp.logical_and(j >= 0, j <= last))
+            def _():
+                @pl.when(n >= 2)
+                def _():
+                    got(half_at[h], j, oc)
+
+                mm(h, wp.at[2 * j + parity], 2 * j + parity)
+
+            return 0
+
+        lax.fori_loop(0, 4, one, 0)
+
+    def spread(j):
+        rc(wo.at[c, 0, j], wo.at[c, 0, j], wx_s.at[j], w_r.at[0, j], xn).wait_recv()
+        rc(wo.at[c, 1, j], wo.at[c, 1, j], wy_s.at[j], w_r.at[1, j], yn).wait_recv()
+
+        @pl.when(j % 2 == 0)
+        def _():
+            d_fx(j).start()
+
+        @pl.when(j % 2 == 1)
+        def _():
+            d_fy(j).start()
+
+    def spread_far(d):
+        for j in (s - d, s + d):
+
+            @pl.when(jnp.logical_and(j >= 0, j <= last))
+            def _():
+                spread(j)
+
+    def settle(h):
+        def one(i, _):
+            r = pl.ds(pl.multiple_of(i * 128, 128), 128)
+            rk = pl.ds(pl.multiple_of(i * 128 + WIN, WIN), 128)
+            p = acc[r, :]
+            q3[h, r, 0:128] = p[:, 0:128].astype(bf)
+            q3[h, r, 128:256] = p[:, 384:512].astype(bf)
+            kv3[h, rk, 0:128] = p[:, 128:256].astype(bf)
+            kv3[h, rk, 128:256] = pltpu.roll(p[:, 384:512], 96, 1).astype(bf)
+            kv3[h, rk, 256:512] = p[:, 256:512].astype(bf)
+            return 0
+
+        lax.fori_loop(0, blocks, one, 0)
+
+        @pl.when(jnp.logical_and(c == 0, jnp.logical_not(has_h)))
+        def _():
+            kv3[h, 0:WIN, :] = jnp.zeros((WIN, 512), bf)
+
+        @pl.when(jnp.logical_and(c == 1, jnp.logical_not(has_h)))
+        def _():
+            kv3[h, rows + WIN : rows + 2 * WIN, :] = jnp.zeros((WIN, 512), bf)
+
+        to_sides(functools.partial(d_h, h))
+
+    def d_h(h, k):
+        src = kv3.at[h, pl.ds(WIN if k == 0 else rows, WIN)]
+        dst = kv3.at[h, pl.ds(rows + WIN if k == 0 else 0, WIN)]
+        return functools.partial(rc, src, dst, h_s.at[h, k], h_r.at[h, 1 - k])
+
+    def wait_sides(d):
+        for k in range(2):
+
+            @pl.when(jnp.logical_or(c == 1 - k, has_h))
+            def _():
+                d(1 - k)(sib).wait_recv()
+
+    lane = lanes(128)
+    scale = math.log2(math.e) / HEAD**0.5
+    zero = jnp.zeros((128, 128), bf)
+    first = (lane < 80, jnp.logical_and(lane >= 32, lane < 112))
+    bufs = (at0, at1)
+
+    def d_a(h, tt, b, sem, way, dev):
+        v = bufs[h].at[tt, b]
+        return rc(v, v, sem.at[h, b], a_r.at[h, way, b], dev)
+
+    def d_af(h, b, by_x):
+        return d_a(h, tx, b, af_s, 2, yn) if by_x else d_a(h, ty, b, af_s, 2, xn)
+
+    def attend(h, b):
+        r = pl.ds(pl.multiple_of(b * 128, 128), 128)
+        rk = pl.ds(pl.multiple_of(b * 128, 128), 256)
+        idq = jnp.transpose(jnp.broadcast_to(idb[1, pl.ds(b, 1), :], (128, 128)))
+        ok = jnp.concatenate([idq == kid[pl.ds(b, 1), :], idq == kid[pl.ds(b + 1, 1), :]], axis=1)
+        qa, qr = q3[h, r, 0:128], q3[h, r, 128:256]
+        parts = (
+            (jnp.where(first[h], qa, zero), 128),
+            (
+                jnp.concatenate(
+                    [jnp.where(first[h], zero, qa), jnp.where(lane < 32, qr, zero)], axis=1
+                ),
+                256,
+            ),
+        )
+        outs = []
+        for q, span in parts:
+            sc = lax.dot_general(
+                q, kv3[h, rk, 0:span], (((1,), (1,)), ((), ())), preferred_element_type=jnp.float32
+            )
+            sc = jnp.where(ok, sc, jnp.float32(-1e30))
+            top = jnp.max(sc, axis=-1, keepdims=True)
+            e = jnp.exp2((sc - top) * scale)
+            total = jnp.sum(e, axis=-1, keepdims=True)
+            o = jnp.dot(e.astype(bf), kv3[h, rk, 256 : 256 + span], preferred_element_type=jnp.float32)
+            outs.append(o * (1.0 / total))
+        o0, o1 = outs
+        nil = jnp.float32(0.0)
+        bufs[h][t, b, 0:128, :] = jnp.where(first[h], o0, o1[:, :128]).astype(bf)
+        more = jnp.where(jnp.logical_and(lane >= 64, lane < 96), o1[:, 128:], nil)
+        if h == 0:
+            rbuf[r, :] = more
+        else:
+            both = rbuf[r, :] + pltpu.roll(more, 32, 1)
+            la = lanes(64)
+            at1[t, b, 128:192, :] = jnp.where(
+                la < 64, pltpu.roll(both[:64], 64, 1), both[64:]
+            ).astype(bf)
+        d_a(h, t, b, ax_s, 0, xn).start()
+        d_a(h, t, b, ay_s, 1, yn).start()
+
+    def relay(h, b):
+        d_a(h, tx, b, ax_s, 0, xn).wait_recv()
+        d_a(h, ty, b, ay_s, 1, yn).wait_recv()
+
+        @pl.when(b % 2 == 0)
+        def _():
+            d_af(h, b, True).start()
+
+        @pl.when(b % 2 == 1)
+        def _():
+            d_af(h, b, False).start()
+
+    def order(i):
+        return jnp.where(i < blocks - 2, i + 1, jnp.where(i == blocks - 2, 0, blocks - 1))
+
+    def attend_at(h, i):
+        @pl.when(i == blocks - 2)
+        def _():
+            wait_sides(functools.partial(d_h, h))
+
+        attend(h, order(i))
+
+    mm_own(0)
+
+    def step0(d, _):
+        pass_on(0, d)
+
+        @pl.when(d == sections // 2)
+        def _():
+            start_own(2)
+
+        mm_far(0, d)
+        pass_on(1, d)
+        return 0
+
+    lax.fori_loop(1, sections, step0, 0)
+    settle(0)
+
+    @pl.when(jnp.logical_and(c == 0, jnp.logical_not(has_h)))
+    def _():
+        idb[0] = jnp.full((8, 128), -1, jnp.int32)
+
+    @pl.when(jnp.logical_and(c == 1, jnp.logical_not(has_h)))
+    def _():
+        idb[2] = jnp.full((8, 128), -1, jnp.int32)
+
+    wait_sides(d_id)
+    chain = jnp.concatenate([idb[0, blocks - 1 : blocks], idb[1, 0:blocks], idb[2, 0:1]], axis=0)
+    after = jnp.concatenate([chain[1:], chain[:1]], axis=0)
+    kid[...] = pltpu.roll(jnp.where(lanes(8) < 64, after, chain), 64, 1)
+
+    mm_own(1)
+    spread(s)
+    per = -(-blocks // (sections - 1))
+
+    def step1(d, _):
+        def some(n, _):
+            i = (d - 1) * per + n
+
+            @pl.when(i < blocks)
+            def _():
+                attend_at(0, i)
+
+                @pl.when(i >= 2)
+                def _():
+                    relay(0, order(i - 2))
+
+            return 0
+
+        lax.fori_loop(0, per, some, 0)
+        pass_on(2, d)
+        spread_far(d)
+        mm_far(1, d)
+        return 0
+
+    lax.fori_loop(1, sections, step1, 0)
+    settle(1)
+
+    def attend_step(i, _):
+        attend_at(1, i)
+
+        @pl.when(i < 2)
+        def _():
+            relay(0, order(i + blocks - 2))
+
+        @pl.when(i == 2)
+        def _():
+            def diag(j, _):
+                rc(wo.at[c, 2, j], wo.at[c, 2, j], wf_s.at[j], w_r.at[2, j], xn).wait_recv()
+                return 0
+
+            lax.fori_loop(0, sections, diag, 0)
+            d_ws().start()
+
+        @pl.when(i >= 2)
+        def _():
+            relay(1, order(i - 2))
+
+        return 0
+
+    lax.fori_loop(0, blocks, attend_step, 0)
+
+    def other(j, _):
+        got(1, j, oc)
+        return 0
+
+    lax.fori_loop(0, sections, other, 0)
+    rc(wo.at[oc], wo.at[oc], ws_s, ws_r, sib).wait_recv()
+
+    def unpack(src, tt, g):
+        at = g * depth
+        wof[tt, pl.ds(pl.multiple_of(at, 16), depth), 0:128] = src[0:depth, :]
+        wof[tt, pl.ds(pl.multiple_of(at, 16), depth), 128:256] = src[depth : 2 * depth, :]
+        h = src[2 * depth : 2 * depth + halfd, :]
+        wof[tt, pl.ds(pl.multiple_of(at, 16), halfd), 256:384] = rot(h, 64)
+        wof[tt, pl.ds(pl.multiple_of(at + halfd, 16), halfd), 256:384] = h
+
+    def unpack_all(j, _):
+        for m in range(2):
+            g = 2 * j + m
+            for k, tt in enumerate((tx, ty, td)):
+                unpack(wo.at[m, k, j], tt, g)
+
+            @pl.when(g != 2 * s + c)
+            def _():
+                unpack(wp.at[g, pl.ds(*region[1])], t, g)
+
+        return 0
+
+    lax.fori_loop(0, sections, unpack_all, 0)
+    unpack(pk.at[pl.ds(*region[1])], t, 2 * s + c)
+
+    def project(i, _):
+        @pl.when(i < 2)
+        def _():
+            relay(1, order(i + blocks - 2))
+
+        b = order(i)
+        r = pl.ds(pl.multiple_of(b * 128, 128), 128)
+        for h in range(2):
+            d_a(h, td, b, af_s, 2, xn).wait_recv()
+        parts = []
+        for k in range(4):
+            f = at1[k, b, 128:192, :].astype(jnp.float32)
+            f = jnp.concatenate([pltpu.roll(f, 64, 1), f], axis=0)
+            parts += [at0[k, b], at1[k, b, 0:128, :]]
+            parts += [jnp.where(lane >= 64, f, jnp.float32(0.0)).astype(bf)]
+        a = jnp.concatenate(parts, axis=1)
+        for n in range(width // 256):
+            w = jnp.concatenate([wof[k, 256 * n : 256 * n + 256, :] for k in range(4)], axis=1)
+            total = lax.dot_general(
+                a, w, (((1,), (1,)), ((), ())), preferred_element_type=jnp.float32
+            )
+            cols = slice(256 * n, 256 * n + 256)
+            out_ref[r, cols] = (x_ref[r, cols].astype(jnp.float32) + total).astype(bf)
+        return 0
+
+    lax.fori_loop(0, blocks, project, 0)
+
+    def sent_w(j, _):
+        for k in range(3):
+
+            @pl.when(jnp.logical_and(has_up, j <= s))
+            def _():
+                d_up(k, j).wait_send()
+
+            @pl.when(jnp.logical_and(has_dn, j >= s))
+            def _():
+                d_dn(k, j).wait_send()
+
+            d_sib(k, j).wait_send()
+        d_wx(j).wait_send()
+        d_wy(j).wait_send()
+        d_fx(j).wait_send()
+        return 0
+
+    lax.fori_loop(0, sections, sent_w, 0)
+    d_ws().wait_send()
+
+    def sent_a(b, _):
+        for h in range(2):
+            d_a(h, t, b, ax_s, 0, xn).wait_send()
+            d_a(h, t, b, ay_s, 1, yn).wait_send()
+            d_af(h, b, True).wait_send()
+        return 0
+
+    lax.fori_loop(0, blocks, sent_a, 0)
+    for d in (d_id, functools.partial(d_h, 0), functools.partial(d_h, 1)):
+        for k in range(2):
+
+            @pl.when(jnp.logical_or(c == 1 - k, has_h))
+            def _():
+                d(k)(sib).wait_send()
+
+
+def fused(sections, patches, window_ids, norm_gain, w_qkv, qkv_bias, w_out):
+    rows, width = patches.shape
+    depth = w_qkv.shape[0]
+    blocks = rows // 128
+    bf, f32, dma = jnp.bfloat16, jnp.float32, pltpu.SemaphoreType.DMA
+    shards = 2 * sections
+    wo_rows = 2 * depth + depth // 2
+    pack_rows = 8 * depth + wo_rows
+    vmem = pl.BlockSpec(memory_space=pltpu.VMEM)
+    return pl.pallas_call(
+        functools.partial(kernel, sections),
+        out_shape=jax.ShapeDtypeStruct((rows, width), bf),
+        in_specs=[vmem] * 6,
+        out_specs=vmem,
+        scratch_shapes=[
+            pltpu.VMEM((4, depth, 384), bf),
+            pltpu.VMEM((8, 384), f32),
+            pltpu.VMEM((pack_rows, 128), bf),
+            pltpu.VMEM((2, 8, 512), f32),
+            pltpu.VMEM((shards, pack_rows, 128), bf),
+            pltpu.VMEM((shards, rows, depth), bf),
+            pltpu.VMEM((rows, 512), f32),
+            pltpu.VMEM((2, rows, 256), bf),
+            pltpu.VMEM((2, rows + 2 * WIN, 512), bf),
+            pltpu.VMEM((rows, 128), f32),
+            pltpu.VMEM((4, blocks, 128, 128), bf),
+            pltpu.VMEM((4, blocks, 192, 128), bf),
+            pltpu.VMEM((2, 3, sections, wo_rows, 128), bf),
+            pltpu.VMEM((4, width, 384), bf),
+            pltpu.VMEM((3, 8, 128), jnp.int32),
+            pltpu.VMEM((8, 128), jnp.int32),
+            dma((3, sections)), dma((3, sections)), dma((3, sections)), dma((3, shards)),
+            dma((sections,)), dma((sections,)), dma((sections,)), dma((3, sections)), dma, dma,
+            dma((2,)), dma((2,)), dma((2, 2)), dma((2, 2)),
+            dma((2, blocks)), dma((2, blocks)), dma((2, blocks)), dma((2, 3, blocks)),
+        ],
+        compiler_params=pltpu.CompilerParams(
+            collective_id=0, has_side_effects=True, vmem_limit_bytes=52 * 1024 * 1024
+        ),
+    )(
+        patches,
+        window_ids.reshape(blocks, 128),
+        norm_gain.reshape(width // 128, 128),
+        jnp.transpose(w_qkv, (1, 0, 2)),
+        w_out,
+        qkv_bias,
+    )
+
+
 def solution(mesh):
     placed = (
         P(("section", "dp"), None),
@@ -80,6 +691,23 @@
         P(None, "tensor"),
         P(("section", "dp"), "tensor"),
     )
+    sections, cores, heads = mesh.shape["section"], mesh.shape["dp"], mesh.shape["tensor"]
+
+    def body(*args):
+        patches, w_qkv = args[0], args[3]
+        rows, width = patches.shape
+        depth = w_qkv.shape[0]
+        fits = (
+            cores == 2
+            and heads == 4
+            and sections % 2 == 0
+            and depth % 32 == 0
+            and w_qkv.shape[2] == 320
+            and width % 256 == 0
+            and rows == 768
+        )
+        return fused(sections, *args) if fits else local(*args)
+
     return jax.shard_map(
-        local, mesh=mesh, in_specs=placed, out_specs=P(("section", "dp"), None), check_vma=False
+        body, mesh=mesh, in_specs=placed, out_specs=P(("section", "dp"), None), check_vma=False
     )

time: 165 us -> 71.7 us (0.43)
  waiting for transfers between devices: 83.2 us -> 0 us
  Pallas kernels: 0 us -> 64.5 us
  blocking collectives: 27.3 us -> 0 us
  between operations: 13.6 us -> 0.01 us
  other arithmetic: 10.9 us -> 0 us
  starting transfers between devices: 7.79 us -> 0 us
  matrix products: 7.75 us -> 0 us
  local copies, waits for them, and re-layouts: 13.7 us -> 6.91 us
    psum x1 -> x0, waiting for transfers between devices: 68.4 us -> none  [local(): lax.psum(partial_out.astype(jnp.bfloat16), 'tensor').astype(jnp.float32)]
    pallas_call x0 -> x1, Pallas kernels: none -> 64.5 us  [fused(): pl.pallas_call(functools.partial(kernel, sections), out_shape=jax.ShapeDt...]
    all_gather x1 -> x0, blocking collectives: 27.3 us -> none  [local(): lax.all_gather(w_out, ('section', 'dp'), axis=0, tiled=True)]
    all_gather x1 -> x0, waiting for transfers between devices: 14.1 us -> none  [local(): piece = lax.all_gather(w_qkv, ('section', 'dp'), axis=0, tiled=True)]
    dot_general x4 -> x0, matrix products: 7.75 us -> none  [the longest x1 3.88 us: local(): jnp.dot(normed, piece.reshape(count, 3 * local_cols), preferred_element_t...]
    ppermute x4 -> x0, starting transfers between devices: 7.75 us -> none  [the longest x2 5.16 us: with_halo(): lax.ppermute(tail, axis, [(i, (i + 1) % count) for i in range(ends)])]
    all_gather x1 -> x0, local copies, waits for them, and re-layouts: 5.29 us -> none  [local(): piece = lax.all_gather(w_qkv, ('section', 'dp'), axis=0, tiled=True)]
    convert_element_type x1 -> x0, other arithmetic: 3.28 us -> none  [local(): return (values_f + summed).astype(jnp.bfloat16)]
  transfers between devices with their start and end apart: 6 -> 0, of which waited for: 2 -> 0; matrix products, arithmetic and copies ran while one was open for 7% -> 0% of each run, Pallas kernels for 0% -> 0%
where the time goes in v2:
time: 71.7 us; the launch traced here: 71.4 us
  Pallas kernels  64.5 us (90%)
  local copies, waits for them, and re-layouts  6.91 us (10%)
    pallas_call x1, Pallas kernels, fused(): pl.pallas_call(functools.partial(kernel, sections), out_shape=jax.ShapeDt...  64.5 us
    unnamed x11, local copies, waits for them, and re-layouts  6.91 us

profile of v2, /device:TPU:0, one launch (start us, length us, event | category | flops | bytes accessed | tf_op | source)
XLA Modules:
  0.0 71.4 jit_solution(14627616226909730279)
XLA Ops:
  0.0 0.0 copy-start
  0.0 1.0 %copy-done = bf16[160,3,320]{2,0,1:T(8,128)(2,1)S(1)} copy-done((bf16[160,3,320]{2,0,1:T(8,128)(2,1)S(1)}, bf16[160,3,320]{2,0,1:T(8,128)(2,1)}, u32[]{:S(2)}) %copy-start) | copy-done | bytes 307224
  1.0 0.0 copy-start.1
  1.0 0.9 %copy-done.1 = bf16[160,320]{1,0:T(8,128)(2,1)S(1)} copy-done((bf16[160,320]{1,0:T(8,128)(2,1)S(1)}, bf16[160,320]{1,0:T(8,128)(2,1)}, u32[]{:S(2)}) %copy-start.1) | copy-done | bytes 102424
  1.9 0.0 copy-start.2
  1.9 0.7 copy-done.2
  2.6 0.0 copy-start.3
  2.6 0.7 copy-done.3
  3.3 0.0 copy-start.4
  3.3 0.7 copy-done.4
  4.0 64.5 %shard_map.64 = bf16[768,1280]{1,0:T(8,128)(2,1)} custom-call(bf16[768,1280]{1,0:T(8,128)(2,1)} %x_ref.1, s32[6,128]{1,0:T(8,128)S(1)} %bitcast.5, f32[10,128]{1,0:T(8,128)S(1)} %bitcast.4, bf16[3,160,320]{2,1,0:T(8,128)(2,1)S(1)} %bitcast.3, bf16[160,320]{1,0:T(8,128)(2,1)S(1)} %copy-done.1, f32[3,320]{1,0:T(4,128)S(1)} %copy-done.3), custom_call_target="tpu_custom_call" | custom-call | tf_op jit(solution)/shard_map/pallas_call | solution.py:645
  68.4 2.9 %copy.8 = bf16[768,1280]{1,0:T(8,128)(2,1)} copy(bf16[768,1280]{1,0:T(8,128)(2,1)} %shard_map.64) | data formatting | bytes 3932160
Async XLA Ops:
  0.0 1.0 %copy-start = (bf16[160,3,320]{2,0,1:T(8,128)(2,1)S(1)}, bf16[160,3,320]{2,0,1:T(8,128)(2,1)}, u32[]{:S(2)}) copy-start(bf16[160,3,320]{2,0,1:T(8,128)(2,1)} %param.9) | copy-start | bytes 921604
  1.0 0.9 %copy-start.1 = (bf16[160,320]{1,0:T(8,128)(2,1)S(1)}, bf16[160,320]{1,0:T(8,128)(2,1)}, u32[]{:S(2)}) copy-start(bf16[160,320]{1,0:T(8,128)(2,1)} %wout_ref.1) | copy-start | bytes 307204
  1.9 0.7 copy-start.2
  2.6 0.7 copy-start.3
  3.3 0.7 copy-start.4

commit v3 on v2

--- a/solution.py
+++ b/solution.py
@@ -83,11 +83,22 @@
 
 def kernel(
     sections,
-    x_ref, ids_ref, gain_ref, w_ref, wout_ref, bias_ref, out_ref,
-    tmp, tmpb, pk, bias, wp, normed, acc, q3, kv3, rbuf, at0, at1, wo, wof, idb, kid,
+    x_in, ids_in, gain_in, w_in, wout_in, bias_in, out_ref,
+    x_ref, ids_ref, gain_ref, w_ref, wout_ref, bias_ref, in_s, tmp, tmpb, pk, bias, wp, normed, acc, q3, kv3, rbuf, at0, at1, wo, wof, idb, kid,
     up_s, dn_s, sib_s, wp_r, wx_s, wy_s, wf_s, w_r, ws_s, ws_r,
     id_s, id_r, h_s, h_r, ax_s, ay_s, af_s, a_r,
 ):
+    incoming = [
+        pltpu.make_async_copy(a, b, in_s.at[i])
+        for i, (a, b) in enumerate(
+            (
+                (w_in, w_ref), (wout_in, wout_ref), (ids_in, ids_ref),
+                (bias_in, bias_ref), (gain_in, gain_ref), (x_in, x_ref),
+            )
+        )
+    ]
+    for copy in incoming:
+        copy.start()
     rows, width = x_ref.shape
     depth = width // (2 * sections)
     halfd = depth // 2
@@ -152,6 +163,8 @@
     def tiles(ref, i):
         return [ref[i, :, 128 * m : 128 * m + 128] for m in range(3)]
 
+    for copy in incoming[:3]:
+        copy.wait()
     for i in range(3):
         tmp[i, :, 256:384] = jnp.zeros((depth, 128), bf)
         tmp[i, :, 0:320] = w_ref[i]
@@ -275,6 +288,8 @@
 
     to_sides(d_id)
 
+    for copy in incoming[3:]:
+        copy.wait()
     tmpb[:, 256:384] = jnp.zeros((8, 128), jnp.float32)
     tmpb[0:3, 0:320] = bias_ref[...]
     bt = [
@@ -465,12 +480,28 @@
     def step0(d, _):
         pass_on(0, d)
 
-        @pl.when(d == sections // 2)
+        @pl.when(d == 1)
         def _():
             start_own(2)
 
+        @pl.when(d < last)
+        def _():
+            pass_on(1, d)
+
         mm_far(0, d)
-        pass_on(1, d)
+
+        @pl.when(d == last)
+        def _():
+            pass_on(1, d)
+
+        @pl.when(d == 1)
+        def _():
+            spread(s)
+
+        @pl.when(d > 1)
+        def _():
+            spread_far(d - 1)
+
         return 0
 
     lax.fori_loop(1, sections, step0, 0)
@@ -489,41 +520,40 @@
     after = jnp.concatenate([chain[1:], chain[:1]], axis=0)
     kid[...] = pltpu.roll(jnp.where(lanes(8) < 64, after, chain), 64, 1)
 
-    mm_own(1)
-    spread(s)
-    per = -(-blocks // (sections - 1))
+    per = -(-blocks // (sections - 2))
+
+    def each(lo, what):
+        def one(n, _):
+            i = lo + n
+
+            @pl.when(jnp.logical_and(i >= 0, i < blocks))
+            def _():
+                what(i)
+
+            return 0
+
+        lax.fori_loop(0, per, one, 0)
+
+    def relay_half0(i):
+        relay(0, order(i))
 
     def step1(d, _):
-        def some(n, _):
-            i = (d - 1) * per + n
-
-            @pl.when(i < blocks)
-            def _():
-                attend_at(0, i)
-
-                @pl.when(i >= 2)
-                def _():
-                    relay(0, order(i - 2))
-
-            return 0
-
-        lax.fori_loop(0, per, some, 0)
-        pass_on(2, d)
-        spread_far(d)
-        mm_far(1, d)
-        return 0
-
-    lax.fori_loop(1, sections, step1, 0)
-    settle(1)
-
-    def attend_step(i, _):
-        attend_at(1, i)
-
-        @pl.when(i < 2)
-        def _():
-            relay(0, order(i + blocks - 2))
-
-        @pl.when(i == 2)
+        @pl.when(d == 1)
+        def _():
+            mm_own(1)
+
+        @pl.when(d < last)
+        def _():
+            pass_on(2, d)
+            each((d - 1) * per, functools.partial(attend_at, 0))
+
+        @pl.when(d == 1)
+        def _():
+            spread_far(last)
+
+        each((d - 2) * per, relay_half0)
+
+        @pl.when(d == last)
         def _():
             def diag(j, _):
                 rc(wo.at[c, 2, j], wo.at[c, 2, j], wf_s.at[j], w_r.at[2, j], xn).wait_recv()
@@ -531,21 +561,13 @@
 
             lax.fori_loop(0, sections, diag, 0)
             d_ws().start()
-
-        @pl.when(i >= 2)
-        def _():
-            relay(1, order(i - 2))
-
+            pass_on(2, d)
+
+        mm_far(1, d)
         return 0
 
-    lax.fori_loop(0, blocks, attend_step, 0)
-
-    def other(j, _):
-        got(1, j, oc)
-        return 0
-
-    lax.fori_loop(0, sections, other, 0)
-    rc(wo.at[oc], wo.at[oc], ws_s, ws_r, sib).wait_recv()
+    lax.fori_loop(1, sections, step1, 0)
+    settle(1)
 
     def unpack(src, tt, g):
         at = g * depth
@@ -567,8 +589,27 @@
 
         return 0
 
-    lax.fori_loop(0, sections, unpack_all, 0)
-    unpack(pk.at[pl.ds(*region[1])], t, 2 * s + c)
+    def attend_step(i, _):
+        attend_at(1, i)
+
+        @pl.when(i >= 2)
+        def _():
+            relay(1, order(i - 2))
+
+        @pl.when(i == blocks - 1)
+        def _():
+            def other(j, _):
+                got(1, j, oc)
+                return 0
+
+            lax.fori_loop(0, sections, other, 0)
+            rc(wo.at[oc], wo.at[oc], ws_s, ws_r, sib).wait_recv()
+            lax.fori_loop(0, sections, unpack_all, 0)
+            unpack(pk.at[pl.ds(*region[1])], t, 2 * s + c)
+
+        return 0
+
+    lax.fori_loop(0, blocks, attend_step, 0)
 
     def project(i, _):
         @pl.when(i < 2)
@@ -645,9 +686,16 @@
     return pl.pallas_call(
         functools.partial(kernel, sections),
         out_shape=jax.ShapeDtypeStruct((rows, width), bf),
-        in_specs=[vmem] * 6,
+        in_specs=[pl.BlockSpec(memory_space=pl.ANY)] * 6,
         out_specs=vmem,
         scratch_shapes=[
+            pltpu.VMEM((rows, width), bf),
+            pltpu.VMEM((blocks, 128), jnp.int32),
+            pltpu.VMEM((width // 128, 128), f32),
+            pltpu.VMEM((3, depth, 320), bf),
+            pltpu.VMEM((depth, 320), bf),
+            pltpu.VMEM((3, 320), f32),
+            dma((6,)),
             pltpu.VMEM((4, depth, 384), bf),
             pltpu.VMEM((8, 384), f32),
             pltpu.VMEM((pack_rows, 128), bf),
@@ -670,7 +718,7 @@
             dma((2, blocks)), dma((2, blocks)), dma((2, blocks)), dma((2, 3, blocks)),
         ],
         compiler_params=pltpu.CompilerParams(
-            collective_id=0, has_side_effects=True, vmem_limit_bytes=52 * 1024 * 1024
+            collective_id=0, has_side_effects=True, vmem_limit_bytes=60 * 1024 * 1024
         ),
     )(
         patches,
@@ -700,6 +748,7 @@
         fits = (
             cores == 2
             and heads == 4
+            and sections >= 4
             and sections % 2 == 0
             and depth % 32 == 0
             and w_qkv.shape[2] == 320

time: 71.7 us -> 66.7 us (0.930)
  local copies, waits for them, and re-layouts: 6.91 us -> 2.94 us
  Pallas kernels: 64.5 us -> 63 us
    unnamed x11 -> x1, local copies, waits for them, and re-layouts: 6.91 us -> 2.94 us
    pallas_call x1, Pallas kernels: 64.5 us -> 63 us  [fused(): pl.pallas_call(functools.partial(kernel, sections), out_shape=jax.ShapeDt...]
where the time goes in v3:
time: 66.7 us; the launch traced here: 66 us
  Pallas kernels  63 us (94%)
  local copies, waits for them, and re-layouts  2.94 us (4%)
    pallas_call x1, Pallas kernels, fused(): pl.pallas_call(functools.partial(kernel, sections), out_shape=jax.ShapeDt...  63 us
    unnamed x1, local copies, waits for them, and re-layouts  2.94 us

profile of v3, /device:TPU:0, one launch (start us, length us, event | category | flops | bytes accessed | tf_op | source)
XLA Modules:
  0.0 66.0 jit_solution(7711734307978858262)
XLA Ops:
  0.0 63.0 %shard_map.64 = bf16[768,1280]{1,0:T(8,128)(2,1)} custom-call(bf16[768,1280]{1,0:T(8,128)(2,1)} %x_in.1, s32[6,128]{1,0:T(8,128)} %bitcast.5, f32[10,128]{1,0:T(8,128)} %bitcast.4, bf16[3,160,320]{2,1,0:T(8,128)(2,1)} %bitcast.3, bf16[160,320]{1,0:T(8,128)(2,1)} %wout_in.1, f32[3,320]{1,0:T(4,128)} %bias_in.1), custom_call_target="tpu_custom_call" | custom-call | tf_op jit(solution)/shard_map/pallas_call | solution.py:686
  63.0 2.9 %copy.8 = bf16[768,1280]{1,0:T(8,128)(2,1)} copy(bf16[768,1280]{1,0:T(8,128)(2,1)} %shard_map.64) | data formatting | bytes 3932160

commit v4 on v3

--- a/solution.py
+++ b/solution.py
@@ -555,13 +555,14 @@
 
         @pl.when(d == last)
         def _():
+            pass_on(2, d)
+
             def diag(j, _):
                 rc(wo.at[c, 2, j], wo.at[c, 2, j], wf_s.at[j], w_r.at[2, j], xn).wait_recv()
                 return 0
 
             lax.fori_loop(0, sections, diag, 0)
             d_ws().start()
-            pass_on(2, d)
 
         mm_far(1, d)
         return 0

time: 66.7 us -> 65.5 us (0.982)
  no operation moved by 1% of the time
where the time goes in v4:
time: 65.5 us; the launch traced here: 65.3 us
  Pallas kernels  62.4 us (95%)
  local copies, waits for them, and re-layouts  2.94 us (4%)
    pallas_call x1, Pallas kernels, fused(): pl.pallas_call(functools.partial(kernel, sections), out_shape=jax.ShapeDt...  62.4 us
    unnamed x1, local copies, waits for them, and re-layouts  2.94 us

profile of v4, /device:TPU:0, one launch (start us, length us, event | category | flops | bytes accessed | tf_op | source)
XLA Modules:
  0.0 65.3 jit_solution(15273283801448596167)
XLA Ops:
  0.0 62.4 %shard_map.64 = bf16[768,1280]{1,0:T(8,128)(2,1)} custom-call(bf16[768,1280]{1,0:T(8,128)(2,1)} %x_in.1, s32[6,128]{1,0:T(8,128)} %bitcast.5, f32[10,128]{1,0:T(8,128)} %bitcast.4, bf16[3,160,320]{2,1,0:T(8,128)(2,1)} %bitcast.3, bf16[160,320]{1,0:T(8,128)(2,1)} %wout_in.1, f32[3,320]{1,0:T(4,128)} %bias_in.1), custom_call_target="tpu_custom_call" | custom-call | tf_op jit(solution)/shard_map/pallas_call | solution.py:687
  62.4 2.9 %copy.8 = bf16[768,1280]{1,0:T(8,128)(2,1)} copy(bf16[768,1280]{1,0:T(8,128)(2,1)} %shard_map.64) | data formatting | bytes 3932160
